TPU v7x, 32 devices: a whole 2x2x4 slice. The times are simulated.
32 devices in a mesh: ctx: 16 (over z, x, core), head: 2 (over y).
Axes of the slice: x: 2, y: 2, z: 4, core: 2. Of those that a mesh axis runs over, the one named last changes fastest.
Arguments:
- queries: bfloat16 [4096, 8192], P('ctx', 'head'), may hold values from -10 to 10
- key_rows: bfloat16 [4096, 1024], P('ctx', 'head'), may hold values from -4.5 to 4.5
- values: bfloat16 [4096, 1024], P('ctx', 'head'), may hold values from -24 to 24
- lengths: int32 [17], replicated, may hold values from 1 to 2304, as said below
- block_plan: int32 [512], P('ctx'), may hold values from 0 to 511, as said below
- inverse: int32 [512], replicated, may hold values from 0 to 511, as said below
- mask_lo: int32 [512], replicated, may hold values from 0 to 511, as said below
- out_weight: bfloat16 [8192, 4096], P('head'), may hold values from -0.375 to 0.375
Outputs:
- mixed_out: bfloat16 [4096, 4096], P('ctx', 'head')
Inputs may be any that keep to these rules, and one draw needn't show every extreme that they name: One document has exactly 2304 tokens, every other is shorter; the lengths sum to 4096. A permutation of the 512 blocks; slot block_plan[b] lies on index block_plan[b] // 32 of ctx; every index receives exactly 32 blocks, and at most 3 blocks of one index go to any one index, which is reached in every draw. inverse[block_plan[b]] == b. mask_lo[b] lies between the block holding the first token of the document of block b's first token and b, both included.
All inputs are finite; a program needn't handle non-finite values.
Results may differ from a plain program's by a relative error of at most 0.02.
Values may be sent and summed in bfloat16 or wider, within the bound.
No kernel may reach another device: no remote copies, remote signals or barrier semaphores. Data moves between devices by JAX's collectives and lax.ppermute only.
A program may use at most 128 MiB of HBM per device.

v0:
```python
import functools

import jax
import jax.numpy as jnp
from jax import lax
from jax.experimental import pallas as pl
from jax.experimental.pallas import tpu as pltpu
from jax.sharding import PartitionSpec as P

HD = 128
BLK = 8
NEG = -1e30
EXP2_SCALE = HD**-0.5 * 1.4426950408889634
FAR = -(1 << 20)
SAFE = 104.0
MIB = 1 << 20
VMEM = pltpu.VMEM
SMALL = pl.CostEstimate(flops=1 << 20, bytes_accessed=1 << 16, transcendentals=0)
LARGE = pl.CostEstimate(flops=1 << 34, bytes_accessed=1 << 27, transcendentals=0)


def shift(array, count, partner):
    pairs = [(i, partner(i)) for i in range(count)]
    return lax.ppermute(array, "ctx", [(i, j) for i, j in pairs if j is not None and 0 <= j < count])


def whole_vmem():
    return pl.BlockSpec(memory_space=VMEM)


def pack_body(ids, key_rows, values, queries, mine, send, sent_queries, keys, vals, sems, *, split):
    core = ids[0] % 2
    rows, width = keys.shape
    half = sent_queries.shape[1]
    theirs = pl.ds(pl.multiple_of((1 - core) * half, half), half)
    copies = [
        pltpu.make_async_copy(key_rows, keys, sems.at[0]),
        pltpu.make_async_copy(values, vals, sems.at[1]),
        pltpu.make_async_copy(queries.at[:, theirs], sent_queries, sems.at[2]),
    ]
    for copy in copies:
        copy.start()
    part = width // split
    copies[0].wait()
    for out, side in ((send, 1 - core), (mine, core)):
        first = pl.multiple_of(side * part if split == 2 else 0, HD)
        for r in range(0, rows, HD):
            for c in range(0, part, HD):
                out[r : r + HD, c : c + HD] = keys[r : r + HD, pl.ds(first + c, HD)].T
    copies[1].wait()
    for out, side in ((send, 1 - core), (mine, core)):
        first = pl.multiple_of(side * part if split == 2 else 0, HD)
        out[:, part:] = vals[:, pl.ds(first, part)]
    copies[2].wait()


def in_hbm(array):
    return pltpu.with_memory_space_constraint(array, pltpu.HBM)


def pack(ids, key_rows, values, queries, split):
    rows, width = key_rows.shape
    out = VMEM((rows, 2 * (width // split)), key_rows.dtype)
    return pl.pallas_call(
        functools.partial(pack_body, split=split),
        out_shape=[out, out, jax.ShapeDtypeStruct((rows, queries.shape[1] // 2), queries.dtype)],
        grid_spec=pltpu.PrefetchScalarGridSpec(
            num_scalar_prefetch=1,
            grid=(1,),
            in_specs=[pl.BlockSpec(memory_space=pl.ANY)] * 3,
            out_specs=[whole_vmem(), whole_vmem(), pl.BlockSpec(memory_space=pl.ANY)],
            scratch_shapes=[
                VMEM((rows, width), key_rows.dtype),
                VMEM((rows, width), key_rows.dtype),
                pltpu.SemaphoreType.DMA((3,)),
            ],
        ),
        compiler_params=pltpu.CompilerParams(vmem_limit_bytes=8 * MIB),
        name="pack",
    )(ids, in_hbm(key_rows), in_hbm(values), in_hbm(queries))


def join_body(ids, mine, other, own, upper):
    rows = mine.shape[0]
    core = ids[0] % 2
    own[pl.ds(pl.multiple_of(core * rows, rows), rows), :] = mine[...]
    own[pl.ds(pl.multiple_of((1 - core) * rows, rows), rows), :] = other[...]
    upper[...] = own[rows:, :]


def join(ids, mine, other):
    rows, width = mine.shape
    return pl.pallas_call(
        join_body,
        out_shape=[
            jax.ShapeDtypeStruct((2 * rows, width), mine.dtype),
            jax.ShapeDtypeStruct((rows, width), mine.dtype),
        ],
        grid_spec=pltpu.PrefetchScalarGridSpec(
            num_scalar_prefetch=1,
            grid=(1,),
            in_specs=[pl.BlockSpec((rows, width), lambda i, s: (0, 0))] * 2,
            out_specs=[
                pl.BlockSpec((2 * rows, width), lambda i, s: (0, 0)),
                pl.BlockSpec((rows, width), lambda i, s: (0, 0)),
            ],
        ),
        compiler_params=pltpu.CompilerParams(vmem_limit_bytes=8 * MIB),
        name="join",
    )(ids, mine, other)


def attend_body(*refs, spans, arrays, group, heads, which, first, fetch, carried, final):
    ids, lows, highs = refs[:3]
    q_own, q_got, start_ref = refs[3:6]
    refs = refs[6:]
    keys, vals, refs = refs[:arrays], refs[arrays : 2 * arrays], refs[2 * arrays + carried :]
    if fetch:
        weight, refs = refs[0], refs[1:]
    acc, top, reach = refs[:3]
    refs = refs[max(carried, 3) :]
    if fetch:
        held_weight, refs = refs[0], refs[1:]
    if final:
        out_ref, refs = refs[0], refs[1:]
    q, some_keys, some_values = refs[:3]

    here = ids[0]
    core, column = here % 2, here // 2 % 2
    rows = q_own.shape[0]
    h = pl.program_id(0)
    t = {"both": lambda: pl.program_id(1), "own": lambda: core, "other": lambda: 1 - core}[which]()
    chip_base = (here - core) * rows
    row_base = chip_base + t * rows
    least, greatest = lows[t], highs[t]

    if fetch:
        columns = held_weight.shape[1]
        first_column = pl.multiple_of(ids[2] * columns, 128)
        copy = pltpu.make_async_copy(weight.at[:, pl.ds(first_column, columns)], held_weight, refs[3])
        pl.when((h == 0) & (pl.program_id(1) == 0))(copy.start)

    bases = [base(chip_base, column, rows) for _, _, _, base in spans]
    runs = [(b + s[2] > least) & (b < row_base + rows) for b, s in zip(bases, spans)]
    fulls = [(b >= greatest) & (b + s[2] <= row_base + 1) for b, s in zip(bases, spans)]

    @pl.when(functools.reduce(jnp.logical_or, runs))
    def _():
        @pl.when(t == core)
        def _():
            for g in range(group):
                q[g] = q_own[:, g * HD : (g + 1) * HD]

        @pl.when(t != core)
        def _():
            for g in range(group):
                q[g] = q_got[:, g * HD : (g + 1) * HD]

    def turned(i):
        array, at, width, _ = spans[i]
        return jnp.concatenate([keys[array][r : r + HD, :] for r in range(at, at + width, HD)], axis=1)

    def with_ones(i):
        array, at, width, _ = spans[i]
        v = vals[array][at : at + width, :]
        return jnp.concatenate([v, jnp.ones((width, HD), v.dtype)], axis=1)

    def bias_of(base, width):
        key_pos = base + lax.broadcasted_iota(jnp.int32, (rows, width), 1)
        row_pos = row_base + lax.broadcasted_iota(jnp.int32, (rows, width), 0)
        starts = jnp.broadcast_to(start_ref[0].astype(jnp.float32), (HD, rows)).T
        starts = jnp.concatenate([starts] * (width // HD), axis=1)
        return jnp.where((key_pos <= row_pos) & (key_pos.astype(jnp.float32) >= starts), 0.0, NEG)

    def row_top(s):
        lane_top = s[:, :HD]
        for i in range(1, s.shape[1] // HD):
            lane_top = jnp.maximum(lane_top, s[:, i * HD : (i + 1) * HD])
        return jnp.max(lane_top, axis=1, keepdims=True)

    def weights_of(s, shift):
        wide = jnp.concatenate([shift] * (s.shape[1] // HD), axis=1)
        return jnp.exp2((s - wide) * EXP2_SCALE).astype(jnp.bfloat16)

    def step(kt, ve, base, mode, unroll):
        masked = base is not None
        if masked:
            bias = bias_of(base, kt.shape[1])

        def one_head(g, carry):
            q_here = q[g]
            s = jnp.dot(q_here, kt, preferred_element_type=jnp.float32)
            if masked:
                s = s + bias
            if mode == "first":
                m = jnp.broadcast_to(row_top(s), (rows, HD))
                top[h, t, g] = m
                acc[h, t, g] = jnp.dot(weights_of(s, m), ve, preferred_element_type=jnp.float32)
                sizes = jnp.abs(q_here.astype(jnp.float32))
                longest = jnp.maximum(carry[0], jnp.max(sizes.reshape(rows // 8, 8, HD), axis=0))
                lowest = jnp.minimum(carry[1], jnp.min(m.reshape(rows // 8, 8, HD), axis=0))
                return longest, lowest
            if mode == "kept":
                acc[h, t, g] += jnp.dot(weights_of(s, top[h, t, g]), ve, preferred_element_type=jnp.float32)
            else:
                m_old = top[h, t, g]
                m = jnp.maximum(m_old, row_top(s))
                fade = jnp.exp2((m_old - m) * EXP2_SCALE)
                update = jnp.dot(weights_of(s, m), ve, preferred_element_type=jnp.float32)
                top[h, t, g] = m
                acc[h, t, g] = acc[h, t, g] * jnp.concatenate([fade, fade], axis=1) + update
            return carry

        def some_heads(at, carry):
            for i in range(unroll):
                carry = one_head(at * unroll + i, carry)
            return carry

        carry = (jnp.zeros((8, HD), jnp.float32), jnp.full((8, HD), -NEG)) if mode == "first" else 0
        carry = lax.fori_loop(0, group // unroll, some_heads, carry)
        if mode == "first":
            reach[h, t, 0], reach[h, t, 1] = carry

    def all_keys(count):
        return jnp.concatenate([turned(i) for i in range(count)], axis=1)

    def all_values(count):
        return jnp.concatenate([with_ones(i) for i in range(count)], axis=0)

    count = len(spans)
    if first:
        pl.when(t == 0)(lambda: step(all_keys(1), all_values(1), bases[0], "first", group))
        pl.when(t == 1)(lambda: step(all_keys(count), all_values(count), bases[0], "first", group))
    else:
        room = jnp.min(reach[h, t, 1]) + SAFE / EXP2_SCALE
        widest = jnp.max(reach[h, t, 0], axis=0, keepdims=True)
        kt = all_keys(count).astype(jnp.float32)
        norms = jnp.max(jnp.sum(kt * kt, axis=0, keepdims=True), axis=1, keepdims=True)
        most = jnp.max(norms * jnp.sum(widest * widest, axis=1, keepdims=True)) * 1.01
        safe = (room > 0.0) & (most <= room * room)
        one_width = len({span[2] for span in spans}) == 1
        together = functools.reduce(jnp.logical_and, fulls) & safe if one_width else False
        if one_width:
            pl.when(together)(lambda: step(all_keys(count), all_values(count), None, "kept", group))

        def alone(chosen, width):
            def one_piece(piece, carry):
                choose = lambda options: functools.reduce(
                    lambda rest, i: jnp.where(piece == i, options[chosen[i]], rest),
                    range(1, len(chosen)),
                    options[chosen[0]],
                )
                base = choose(bases)
                run = choose([jnp.int32(r) for r in runs]) == 1

                @pl.when(run)
                def _():
                    for i, span in enumerate(chosen):

                        @pl.when(piece == i)
                        def _(span=span):
                            some_keys[:, :width] = turned(span)
                            some_values[:width] = with_ones(span)

                def part(base, mode, unroll):
                    return lambda: step(some_keys[:, :width], some_values[:width], base, mode, unroll)

                masked = run & safe
                if one_width:
                    full = choose([jnp.int32(f) for f in fulls]) == 1
                    pl.when(masked & full)(part(None, "kept", group))
                    masked = masked & jnp.logical_not(full)
                pl.when(masked)(part(base, "kept", group))
                pl.when(run & jnp.logical_not(safe))(part(base, "moved", 1))
                return carry

            lax.fori_loop(0, len(chosen), one_piece, 0)

        @pl.when(jnp.logical_not(together))
        def _():
            for width in sorted({span[2] for span in spans}):
                alone([i for i in range(count) if spans[i][2] == width], width)

    if fetch:
        pl.when((h == heads - 1) & (pl.program_id(1) == pl.num_programs(1) - 1))(copy.wait)
    if final:
        for g in range(group):
            a = acc[h, t, g]
            out_ref[:, g * HD : (g + 1) * HD] = (a[:, :HD] / a[:, HD:]).astype(jnp.bfloat16)


def attend(scalars, queries, got_queries, starts, pieces, spans, state, group, heads, which, weight=None, columns=0):
    rows, width = queries.shape[0], group * HD
    first, fetch, final = state is None, weight is not None, which != "both"
    tiles = 2 if which == "both" else 1

    def tile_of(t, ids):
        return {"both": t, "own": ids[0] % 2, "other": 1 - ids[0] % 2}[which]

    in_specs = [
        pl.BlockSpec((rows, width), lambda h, t, i, *_: (0, i[0] % 2 * heads + h)),
        pl.BlockSpec((rows, width), lambda h, t, *_: (0, h)),
        pl.BlockSpec((1, 1, rows), lambda h, t, i, *_: (tile_of(t, i), 0, 0)),
    ]
    in_specs += [pl.BlockSpec((p.shape[0], HD), lambda h, t, *_: (0, h)) for p in pieces]
    in_specs += [pl.BlockSpec((p.shape[0], HD), lambda h, t, *_: (0, heads + h)) for p in pieces]
    operands = [*scalars, in_hbm(queries), got_queries, starts, *pieces, *pieces]
    out_shape = [
        VMEM((heads, 2, group, rows, 2 * HD), jnp.float32),
        VMEM((heads, 2, group, rows, HD), jnp.float32),
        VMEM((heads, 2, 2, 8, HD), jnp.float32),
    ]
    aliases = {}
    if not first:
        out_shape = [VMEM(a.shape, a.dtype) for a in state]
        aliases = {len(operands) + i: i for i in range(len(state))}
        operands += state
        in_specs += [whole_vmem()] * len(state)
    out_specs = [whole_vmem()] * len(out_shape)
    wide = max(span[2] for span in spans)
    scratch = [
        VMEM((group, rows, HD), queries.dtype),
        VMEM((HD, wide), queries.dtype),
        VMEM((wide, 2 * HD), queries.dtype),
    ]
    if fetch:
        operands.append(weight)
        in_specs.append(pl.BlockSpec(memory_space=pl.ANY))
        out_shape.append(VMEM((weight.shape[0], columns), weight.dtype))
        out_specs.append(whole_vmem())
        scratch.append(pltpu.SemaphoreType.DMA)
    if final:
        out_shape.append(jax.ShapeDtypeStruct((rows, heads * width), queries.dtype))
        out_specs.append(pl.BlockSpec((rows, width), lambda h, t, *_: (0, h)))
    keys = sum(s[2] for s in spans)
    return pl.pallas_call(
        functools.partial(
            attend_body,
            spans=spans,
            arrays=len(pieces),
            group=group,
            heads=heads,
            which=which,
            first=first,
            fetch=fetch,
            carried=0 if first else len(state),
            final=final,
        ),
        out_shape=out_shape,
        grid_spec=pltpu.PrefetchScalarGridSpec(
            num_scalar_prefetch=3,
            grid=(heads, tiles),
            in_specs=in_specs,
            out_specs=out_specs,
            scratch_shapes=scratch,
        ),
        input_output_aliases=aliases,
        compiler_params=pltpu.CompilerParams(vmem_limit_bytes=14 * MIB),
        cost_estimate=SMALL,
        name=f"attend_{which}_{keys}",
    )(*operands)


def project_held_body(ids, a_ref, b_ref, w_ref, alias, o_ref, *, at, tile):
    half = a_ref.shape[1]
    core = ids[0] % 2
    mine = pl.ds(pl.multiple_of(core * half, half), half)
    theirs = pl.ds(pl.multiple_of((1 - core) * half, half), half)
    for n in range(o_ref.shape[1] // tile):
        cols = slice(at + n * tile, at + (n + 1) * tile)
        total = jnp.dot(a_ref[...], w_ref[mine, cols], preferred_element_type=jnp.float32)
        total = total + jnp.dot(b_ref[...], w_ref[theirs, cols], preferred_element_type=jnp.float32)
        o_ref[:, n * tile : (n + 1) * tile] = total.astype(o_ref.dtype)


def project_held(ids, a, b, held, at, columns):
    rows, half = a.shape
    block = lambda shape: pl.BlockSpec(shape, lambda i, s: (0, 0))
    return pl.pallas_call(
        functools.partial(project_held_body, at=at, tile=min(256, columns)),
        out_shape=[VMEM(held.shape, held.dtype), jax.ShapeDtypeStruct((rows, columns), a.dtype)],
        grid_spec=pltpu.PrefetchScalarGridSpec(
            num_scalar_prefetch=1,
            grid=(1,),
            in_specs=[block((rows, half)), block((rows, half)), whole_vmem()],
            out_specs=[whole_vmem(), block((rows, columns))],
        ),
        input_output_aliases={3: 0},
        compiler_params=pltpu.CompilerParams(vmem_limit_bytes=16 * MIB),
        cost_estimate=pl.CostEstimate(flops=4 * rows * half * columns, bytes_accessed=64 * MIB, transcendentals=0),
        name="project_held",
    )(ids, a, b, held)


def project_body(ids, a_ref, b_ref, wa_ref, wb_ref, o_ref):
    total = jnp.dot(a_ref[...], wa_ref[...], preferred_element_type=jnp.float32)
    total = total + jnp.dot(b_ref[...], wb_ref[...], preferred_element_type=jnp.float32)
    o_ref[...] = total.astype(o_ref.dtype)


def project(ids, a, b, weight, columns, at, chosen, tile):
    rows, half = a.shape
    first = lambda s: (s[1] * columns + at) // tile
    block = pl.BlockSpec((rows, half), lambda n, s: (0, 0))
    return pl.pallas_call(
        project_body,
        out_shape=jax.ShapeDtypeStruct((rows, chosen), a.dtype),
        grid_spec=pltpu.PrefetchScalarGridSpec(
            num_scalar_prefetch=1,
            grid=(chosen // tile,),
            in_specs=[
                block,
                block,
                pl.BlockSpec((half, tile), lambda n, s: (s[0] % 2, first(s) + n)),
                pl.BlockSpec((half, tile), lambda n, s: (1 - s[0] % 2, first(s) + n)),
            ],
            out_specs=pl.BlockSpec((rows, tile), lambda n, s: (0, n)),
        ),
        compiler_params=pltpu.CompilerParams(vmem_limit_bytes=48 * MIB),
        cost_estimate=LARGE if at else SMALL,
        name="project",
    )(ids, a, b, weight, weight)


def add_body(kept, arrived, *refs):
    refs[-1][...] = (kept[...].astype(jnp.float32) + arrived[...].astype(jnp.float32)).astype(refs[-1].dtype)


def add_columns(kept, arrived, columns, at, before):
    rows, tile = kept.shape[0], 512
    block = pl.BlockSpec((rows, tile), lambda n: (0, n))
    return pl.pallas_call(
        add_body,
        out_shape=jax.ShapeDtypeStruct((rows, columns), kept.dtype),
        grid=(kept.shape[1] // tile,),
        in_specs=[block, block] + [pl.BlockSpec(memory_space=pl.ANY)] * len(before),
        out_specs=pl.BlockSpec((rows, tile), lambda n: (0, at // tile + n)),
        input_output_aliases={2: 0} if before else {},
        compiler_params=pltpu.CompilerParams(vmem_limit_bytes=8 * MIB),
        cost_estimate=SMALL,
        name="add_columns",
    )(kept, arrived, *before)


def on_device(queries, key_rows, values, lengths, block_plan, inverse, mask_lo, out_weight):
    rows, query_width = queries.shape
    kv_heads = key_rows.shape[1] // HD
    count, head_count = lax.axis_size("ctx"), lax.axis_size("head")
    here, head_here = lax.axis_index("ctx"), lax.axis_index("head")
    core = here % 2
    split = 2 if kv_heads % 2 == 0 else 1
    heads = kv_heads // split
    half = query_width // 2
    group = half // (heads * HD)
    levels = count // 8

    place = jnp.arange(3, dtype=jnp.int32)
    send_half = 1 - head_here if head_count == 2 else 0
    ids = jnp.where(place == 0, here, jnp.where(place == 1, head_here, send_half)).astype(jnp.int32)

    sibling = functools.partial(shift, count=count, partner=lambda i: i ^ 1)
    mine, send, sent_queries = pack(ids, key_rows, values, queries, split)
    swapped = sibling(send)
    up_level = functools.partial(shift, count=count, partner=lambda i: i + 4)
    first_hop = [up_level(mine), up_level(swapped)]
    own, upper = join(ids, mine, swapped)
    sent_queries, lengths, mask_lo, _ = lax.optimization_barrier((sent_queries, lengths, mask_lo, swapped))
    got_queries = sibling(sent_queries)

    chip_base = (here - core) * rows
    doc_ends = jnp.cumsum(lengths)
    pos = chip_base + jnp.arange(2 * rows, dtype=jnp.int32)
    doc_start = jnp.max(jnp.where(doc_ends[None, :] <= pos[:, None], doc_ends[None, :], 0), axis=1)
    low = lax.dynamic_slice_in_dim(mask_lo, chip_base // BLK, 2 * rows // BLK) * BLK
    starts = jnp.maximum(doc_start, jnp.repeat(low, BLK)).astype(jnp.int32).reshape(2, rows)
    scalars = (ids, jnp.min(starts, axis=1), jnp.max(starts, axis=1))
    start_rows = starts[:, None, :]

    common = (scalars, queries, got_queries, start_rows)
    near = shift(own, count, lambda i: i + 2 if i // 2 % 2 == 0 else None)
    own_spans = [(0, 0, rows, lambda base, column, r: base), (0, rows, rows, lambda base, column, r: base + r)]
    state = attend(*common, [own], own_spans, None, group, heads, "both")
    keep = out_weight.shape[1] // head_count
    held_columns = keep if head_count == 2 else out_weight.shape[1]

    before, at_before = near, lambda base, column, r: jnp.where(column == 1, base - 2 * r, FAR)
    for d in range(1, levels + 1):
        if d == 1:
            first_hop = lax.optimization_barrier((*first_hop, state[2]))[:2]
            moving, _ = join(ids, *first_hop)
        else:
            moving, _ = lax.optimization_barrier((moving, state[2]))
        at_level = lambda base, column, r, d=d: base - 4 * d * r
        if d < levels:
            crossed = shift(moving, count, lambda i: i ^ 2)
            at_cross = lambda base, column, r, d=d: base - 4 * d * r + jnp.where(column == 0, 2 * r, -2 * r)
        else:
            crossed = shift(moving, count, lambda i: i - 2 if i // 2 % 2 == 1 else None)
            at_cross = lambda base, column, r, d=d: jnp.where(column == 0, base - 4 * d * r + 2 * r, FAR)
        onward = shift(moving, count, lambda i: i + 4) if d < levels else None
        if d == 1:
            reach = 4 * levels + 2
            upper, _ = lax.optimization_barrier((upper, moving))
            farthest = shift(upper, count, lambda i: i + reach)
        spans = [(0, 0, 2 * rows, at_before), (1, 0, 2 * rows, at_level)]
        fetch = (out_weight, held_columns) if d == levels else ()
        state = attend(*common, [before, moving], spans, state, group, heads, "both", *fetch)
        before, at_before, moving = crossed, at_cross, onward
    at_farthest = lambda base, column, r: base - reach * r + r
    spans = [(0, 0, 2 * rows, at_before), (1, 0, rows, at_farthest)]
    *state, theirs = attend(*common, [before, farthest], spans, state, group, heads, "other")
    got = sibling(theirs)
    *state, att = attend(*common, [before, farthest], spans, state, group, heads, "own")
    held = state[3]

    if head_count != 2:
        _, partial_sums = project_held(ids, att, got, held, 0, held_columns)
        return lax.psum_scatter(partial_sums, "head", scatter_dimension=1, tiled=True)
    parts = ((0, keep // 4), (keep // 4, keep // 2), (3 * keep // 4, keep // 4))
    arrived = []
    for at, columns in parts:
        held, sent = project_held(ids, att, got, held, at, columns)
        arrived.append(lax.ppermute(sent, "head", [(0, 1), (1, 0)]))
    out = []
    for (at, columns), part in zip(parts, arrived):
        kept = project(ids, att, got, out_weight, keep, at, columns, 256)
        out = [add_columns(kept, part, keep, at, out)]
        ids, _ = lax.optimization_barrier((ids, out[0]))
    return out[0]


def solution(mesh):
    in_specs = (
        P("ctx", "head"),
        P("ctx", "head"),
        P("ctx", "head"),
        P(),
        P("ctx"),
        P(),
        P(),
        P("head", None),
    )
    return jax.shard_map(
        on_device, mesh=mesh, in_specs=in_specs, out_specs=P("ctx", "head"), check_vma=False
    )
```

profile of v0, /device:TPU:16, one launch (start us, length us, event | category | flops | bytes accessed | tf_op | source)
XLA Modules:
  0.0 131.6 jit_solution(17874746447545188166)
XLA Ops:
  0.0 2.0 %pack.1 = (bf16[256,512]{1,0:T(8,128)(2,1)S(1)}, bf16[256,512]{1,0:T(8,128)(2,1)S(1)}, bf16[256,2048]{1,0:T(8,128)(2,1)S(1)}) custom-call(s32[3]{0:T(128)S(1)} %compare_select_fusion.1.ids.refs_0_, bf16[256,512]{1,0:T(8,128)(2,1)} %key_rows.1, bf16[256,512]{1,0:T(8,128)(2,1)} %values.1, bf16[256,4096]{1,0:T(8,128)(2,1)} %refs_3_.9), custom_call_target="tpu_custom_call" | custom-call | tf_op jit(solution)/shard_map/pack/pallas_call | solution.py:64
  2.0 1.5 %collective-permute-done.other = bf16[256,512]{1,0:T(8,128)(2,1)S(1)} collective-permute-done((bf16[256,512]{1,0:T(8,128)(2,1)S(1)}, bf16[256,512]{1,0:T(8,128)(2,1)S(1)}, u32[]{:S(2)}, u32[]{:S(2)}) %collective-permute-start) | collective-permute-done | bytes 262176 | tf_op jit(solution)/shard_map/ppermute | solution.py:24
  3.7 3.5 %collective-permute-start.2 = (bf16[256,512]{1,0:T(8,128)(2,1)S(1)}, bf16[256,512]{1,0:T(8,128)(2,1)S(1)}, u32[]{:S(2)}, u32[]{:S(2)}) collective-permute-start(bf16[256,512]{1,0:T(8,128)(2,1)S(1)} %get-tuple-element.47.mine), channel_id=1, source_target_pairs={{0,8},{2,10},{4,12},{6,14},{8,16},{10,18},{12,20},{14,22},{16,24},... | collective-permute-start | bytes 786440 | tf_op jit(solution)/shard_map/ppermute | solution.py:24
  7.3 1.9 %collective-permute-start.3 = (bf16[256,512]{1,0:T(8,128)(2,1)S(1)}, bf16[256,512]{1,0:T(8,128)(2,1)S(1)}, u32[]{:S(2)}, u32[]{:S(2)}) collective-permute-start(bf16[256,512]{1,0:T(8,128)(2,1)S(1)} %collective-permute-done.other), channel_id=1, source_target_pairs={{0,8},{2,10},{4,12},{6,14},{8,16},{10,18},{12,20},{14,22},{16,24},... | collective-permute-start | bytes 786440 | tf_op jit(solution)/shard_map/ppermute | solution.py:24
  11.9 3.4 %collective-permute-start.5 = (bf16[512,512]{1,0:T(8,128)(2,1)S(1)}, bf16[512,512]{1,0:T(8,128)(2,1)S(1)}, u32[]{:S(2)}, u32[]{:S(2)}) collective-permute-start(bf16[512,512]{1,0:T(8,128)(2,1)S(1)} %get-tuple-element.48.refs_6_.refs_7_), channel_id=1, source_target_pairs={{0,4},{2,6},{8,12},{10,14},{16,20},{18,22},{24,28},{26,30},{1,5},{... | collective-permute-start | bytes 1572872 | tf_op jit(solution)/shard_map/ppermute | solution.py:24
  15.5 7.9 %attend_both_512.1 = (f32[2,2,8,256,256]{4,3,2,1,0:T(8,128)S(1)}, f32[2,2,8,256,128]{4,3,2,1,0:T(8,128)S(1)}, f32[2,2,2,8,128]{4,3,2,1,0:T(8,128)S(1)}) custom-call(s32[3]{0:T(128)S(1)} %compare_select_fusion.1.ids.refs_0_, s32[2]{0:T(128)S(1)} %get-tuple-element.80.refs_1_, s32[2]{0:T(128)S(1)} %get-tuple-element.79.refs_2_, bf16[256,4096]{1,0:T(8,128)(2,1)} %refs_3_.9, ...), custom_call_target="tpu_custom_call" | custom-call | flops 1048576 | bytes 65536 | tf_op jit(solution)/shard_map/attend_both_512/pallas_call | solution.py:336
  23.4 1.3 join.3
  24.7 1.9 %collective-permute-start.4 = (bf16[512,512]{1,0:T(8,128)(2,1)S(1)}, bf16[512,512]{1,0:T(8,128)(2,1)S(1)}, u32[]{:S(2)}, u32[]{:S(2)}) collective-permute-start(bf16[512,512]{1,0:T(8,128)(2,1)S(1)} %get-tuple-element.52.refs_7_.refs_9_), channel_id=1, source_target_pairs={{0,8},{2,10},{4,12},{6,14},{8,16},{10,18},{12,20},{14,22},{16,24},... | collective-permute-start | bytes 1572872 | tf_op jit(solution)/shard_map/ppermute | solution.py:24
  26.8 18.7 %attend_both_1024.2 = (f32[2,2,8,256,256]{4,3,2,1,0:T(8,128)S(1)}, f32[2,2,8,256,128]{4,3,2,1,0:T(8,128)S(1)}, f32[2,2,2,8,128]{4,3,2,1,0:T(8,128)S(1)}) custom-call(s32[3]{0:T(128)S(1)} %compare_select_fusion.1.ids.refs_0_, s32[2]{0:T(128)S(1)} %get-tuple-element.80.refs_1_, ...), custom_call_target="tpu_custom_call", output_to_operand_aliasing={{0}: (10, {}), {1}: (11, {}), {2}: (12, {})} | custom-call | flops 1048576 | bytes 65536 | tf_op jit(solution)/shard_map/attend_both_1024/pallas_call | solution.py:336
  45.5 1.3 collective-permute-start.6
  46.8 0.9 collective-permute-start.7
  47.7 34.0 %attend_both_1024.3 = (f32[2,2,8,256,256]{4,3,2,1,0:T(8,128)S(1)}, f32[2,2,8,256,128]{4,3,2,1,0:T(8,128)S(1)}, f32[2,2,2,8,128]{4,3,2,1,0:T(8,128)S(1)}, bf16[4096,2048]{1,0:T(8,128)(2,1)S(1)}) custom-call(s32[3]{0:T(128)S(1)} %compare_select_fusion.1.ids.refs_0_, ...), custom_call_target="tpu_custom_call", output_to_operand_aliasing={{0}: (10, {}), {1}: (11, {}), {2}: (12, {})} | custom-call | flops 1048576 | bytes 65536 | tf_op jit(solution)/shard_map/attend_both_1024/pallas_call | solution.py:336
  81.7 10.3 %attend_other_768.1 = (f32[2,2,8,256,256]{4,3,2,1,0:T(8,128)S(1)}, f32[2,2,8,256,128]{4,3,2,1,0:T(8,128)S(1)}, f32[2,2,2,8,128]{4,3,2,1,0:T(8,128)S(1)}, bf16[40...) custom-call(s32[3]{0:T(128)S(1)} %compare_select_fusion.1.ids.refs_0, ...), custom_call_target="tpu_custom_call", output_to_operand_aliasing={{0}: (10, {}), {1}: (11, {}), {2}: (12, {}), {3}: (13, {})} | custom-call | flops 1048576 | bytes 65536 | tf_op jit(solution)/shard_map/attend_other_768/pallas_call | solution.py:336
  92.1 10.5 %attend_own_768.1 = (f32[2,2,8,256,256]{4,3,2,1,0:T(8,128)S(1)}, f32[2,2,8,256,128]{4,3,2,1,0:T(8,128)S(1)}, f32[2,2,2,8,128]{4,3,2,1,0:T(8,128)S(1)}, bf16[4096...) custom-call(s32[3]{0:T(128)S(1)} %compare_select_fusion.1.ids.refs_0, ...), custom_call_target="tpu_custom_call", output_to_operand_aliasing={{0}: (10, {}), {1}: (11, {}), {2}: (12, {}), {3}: (13, {})} | custom-call | flops 1048576 | bytes 65536 | tf_op jit(solution)/shard_map/attend_own_768/pallas_call | solution.py:336
  102.6 2.5 %project_held.3 = (bf16[4096,2048]{1,0:T(8,128)(2,1)S(1)}, bf16[256,512]{1,0:T(8,128)(2,1)}) custom-call(s32[3]{0:T(128)S(1)} %compare_select_fusion.1.ids.refs_0_, bf16[256,2048]{1,0:T(8,128)(2,1)S(1)} %get-tuple-element.69.a_ref, bf16[256,2048]{1,0:T(8,128)(2,1)S(1)} %collective-permute-done.9.b_ref, ...), custom_call_target="tpu_custom_call", output_to_operand_aliasing={{0}: (3, {})} | custom-call | flops 1073741824 | bytes 67108864 | tf_op jit(solution)/shard_map/project_held/pallas_call | solution.py:379
  105.1 1.5 %collective-permute-start.10 = (bf16[256,512]{1,0:T(8,128)(2,1)}, bf16[256,512]{1,0:T(8,128)(2,1)S(1)}, u32[]{:S(2)}, u32[]{:S(2)}) collective-permute-start(bf16[256,512]{1,0:T(8,128)(2,1)} %get-tuple-element.72), channel_id=1, source_target_pairs={{0,1},{1,0},{2,3},{3,2},{4,5},{5,4},{6,7},{7,6},{8,9},{9,8},{10,11... | collective-permute-start | bytes 786440 | tf_op jit(solution)/shard_map/ppermute | solution.py:523
  106.6 3.7 %project_held.4 = (bf16[4096,2048]{1,0:T(8,128)(2,1)S(1)}, bf16[256,1024]{1,0:T(8,128)(2,1)}) custom-call(s32[3]{0:T(128)S(1)} %compare_select_fusion.1.ids.refs_0_, bf16[256,2048]{1,0:T(8,128)(2,1)S(1)} %get-tuple-element.69.a_ref, bf16[256,2048]{1,0:T(8,128)(2,1)S(1)} %collective-permute-done.9.b_ref, ...), custom_call_target="tpu_custom_call", output_to_operand_aliasing={{0}: (3, {})} | custom-call | flops 2147483648 | bytes 67108864 | tf_op jit(solution)/shard_map/project_held/pallas_call | solution.py:379
  110.8 1.8 %project_held.5 = (bf16[4096,2048]{1,0:T(8,128)(2,1)S(1)}, bf16[256,512]{1,0:T(8,128)(2,1)S(1)}) custom-call(s32[3]{0:T(128)S(1)} %compare_select_fusion.1.ids.refs_0_, bf16[256,2048]{1,0:T(8,128)(2,1)S(1)} %get-tuple-element.69.a_ref, bf16[256,2048]{1,0:T(8,128)(2,1)S(1)} %collective-permute-done.9.b_ref, ...), custom_call_target="tpu_custom_call", output_to_operand_aliasing={{0}: (3, {})} | custom-call | flops 1073741824 | bytes 67108864 | tf_op jit(solution)/shard_map/project_held/pallas_call | solution.py:379
  112.6 1.6 %collective-permute-start.12 = (bf16[256,512]{1,0:T(8,128)(2,1)S(1)}, bf16[256,512]{1,0:T(8,128)(2,1)S(1)}, u32[]{:S(2)}, u32[]{:S(2)}) collective-permute-start(bf16[256,512]{1,0:T(8,128)(2,1)S(1)} %get-tuple-element.78), channel_id=1, source_target_pairs={{0,1},{1,0},{2,3},{3,2},{4,5},{5,4},{6,7},{7,6},{8,9},{9,8},{10,11... | collective-permute-start | bytes 786440 | tf_op jit(solution)/shard_map/ppermute | solution.py:523
  114.2 3.6 %project.3.kept = bf16[256,512]{1,0:T(8,128)(2,1)S(1)} custom-call(s32[3]{0:T(128)S(1)} %compare_select_fusion.1.ids.refs_0_, bf16[256,2048]{1,0:T(8,128)(2,1)S(1)} %get-tuple-element.69.a_ref, bf16[256,2048]{1,0:T(8,128)(2,1)S(1)} %collective-permute-done.9.b_ref, bf16[4096,4096]{1,0:T(8,128)(2,1)} %wb_ref.5, bf16[4096,4096]{1,0:T(8,128)(2,1)} %wb_ref.5), custom_call_target="tpu_custom_call" | custom-call | flops 1048576 | bytes 65536 | tf_op jit(solution)/shard_map/project/pallas_call | solution.py:405
  118.6 6.1 %project.4.kept = bf16[256,1024]{1,0:T(8,128)(2,1)S(1)} custom-call(s32[3]{0:T(128)S(1)} %compare_select_fusion.1.ids.refs_0_, bf16[256,2048]{1,0:T(8,128)(2,1)S(1)} %get-tuple-element.69.a_ref, bf16[256,2048]{1,0:T(8,128)(2,1)S(1)} %collective-permute-done.9.b_ref, bf16[4096,4096]{1,0:T(8,128)(2,1)} %wb_ref.5, bf16[4096,4096]{1,0:T(8,128)(2,1)} %wb_ref.5), custom_call_target="tpu_custom_call" | custom-call | flops 17179869184 | bytes 134217728 | tf_op jit(solution)/shard_map/project/pallas_call | solution.py:405
  124.7 1.0 collective-permute-done.11.arrived
  125.7 0.9 add_columns.4.refs_0_
  126.6 3.6 %project.5.kept = bf16[256,512]{1,0:T(8,128)(2,1)S(1)} custom-call(s32[3]{0:T(128)S(1)} %compare_select_fusion.1.ids.refs_0_, bf16[256,2048]{1,0:T(8,128)(2,1)S(1)} %get-tuple-element.69.a_ref, bf16[256,2048]{1,0:T(8,128)(2,1)S(1)} %collective-permute-done.9.b_ref, bf16[4096,4096]{1,0:T(8,128)(2,1)} %wb_ref.5, bf16[4096,4096]{1,0:T(8,128)(2,1)} %wb_ref.5), custom_call_target="tpu_custom_call" | custom-call | flops 17179869184 | bytes 134217728 | tf_op jit(solution)/shard_map/project/pallas_call | solution.py:405
  (33 shorter events, 5.9 us)
Async XLA Ops:
  2.0 1.6 %collective-permute-start = (bf16[256,512]{1,0:T(8,128)(2,1)S(1)}, bf16[256,512]{1,0:T(8,128)(2,1)S(1)}, u32[]{:S(2)}, u32[]{:S(2)}) collective-permute-start(bf16[256,512]{1,0:T(8,128)(2,1)S(1)} %get-tuple-element.43), channel_id=1, source_target_pairs={{0,2},{2,0},{4,6},{6,4},{8,10},{10,8},{12,14},{14,12},{16,18},{18,... | collective-permute-start | bytes 786440 | tf_op jit(solution)/shard_map/ppermute | solution.py:24
  3.6 11.9 %collective-permute-start.1 = (bf16[256,2048]{1,0:T(8,128)(2,1)S(1)}, bf16[256,2048]{1,0:T(8,128)(2,1)S(1)}, u32[]{:S(2)}, u32[]{:S(2)}) collective-permute-start(bf16[256,2048]{1,0:T(8,128)(2,1)S(1)} %get-tuple-element.46), channel_id=1, source_target_pairs={{0,2},{2,0},{4,6},{6,4},{8,10},{10,8},{12,14},{14,12},{16,18},{18,... | collective-permute-start | bytes 3145736 | tf_op jit(solution)/shard_map/ppermute | solution.py:24
  3.7 19.7 %collective-permute-start.2 = (bf16[256,512]{1,0:T(8,128)(2,1)S(1)}, bf16[256,512]{1,0:T(8,128)(2,1)S(1)}, u32[]{:S(2)}, u32[]{:S(2)}) collective-permute-start(bf16[256,512]{1,0:T(8,128)(2,1)S(1)} %get-tuple-element.47.mine), channel_id=1, source_target_pairs={{0,8},{2,10},{4,12},{6,14},{8,16},{10,18},{12,20},{14,22},{16,24},... | collective-permute-start | bytes 786440 | tf_op jit(solution)/shard_map/ppermute | solution.py:24
  7.3 16.2 %collective-permute-start.3 = (bf16[256,512]{1,0:T(8,128)(2,1)S(1)}, bf16[256,512]{1,0:T(8,128)(2,1)S(1)}, u32[]{:S(2)}, u32[]{:S(2)}) collective-permute-start(bf16[256,512]{1,0:T(8,128)(2,1)S(1)} %collective-permute-done.other), channel_id=1, source_target_pairs={{0,8},{2,10},{4,12},{6,14},{8,16},{10,18},{12,20},{14,22},{16,24},... | collective-permute-start | bytes 786440 | tf_op jit(solution)/shard_map/ppermute | solution.py:24
  11.9 14.8 %collective-permute-start.5 = (bf16[512,512]{1,0:T(8,128)(2,1)S(1)}, bf16[512,512]{1,0:T(8,128)(2,1)S(1)}, u32[]{:S(2)}, u32[]{:S(2)}) collective-permute-start(bf16[512,512]{1,0:T(8,128)(2,1)S(1)} %get-tuple-element.48.refs_6_.refs_7_), channel_id=1, source_target_pairs={{0,4},{2,6},{8,12},{10,14},{16,20},{18,22},{24,28},{26,30},{1,5},{... | collective-permute-start | bytes 1572872 | tf_op jit(solution)/shard_map/ppermute | solution.py:24
  24.7 20.8 %collective-permute-start.4 = (bf16[512,512]{1,0:T(8,128)(2,1)S(1)}, bf16[512,512]{1,0:T(8,128)(2,1)S(1)}, u32[]{:S(2)}, u32[]{:S(2)}) collective-permute-start(bf16[512,512]{1,0:T(8,128)(2,1)S(1)} %get-tuple-element.52.refs_7_.refs_9_), channel_id=1, source_target_pairs={{0,8},{2,10},{4,12},{6,14},{8,16},{10,18},{12,20},{14,22},{16,24},... | collective-permute-start | bytes 1572872 | tf_op jit(solution)/shard_map/ppermute | solution.py:24
  26.7 21.0 %collective-permute-start.8 = (bf16[512,512]{1,0:T(8,128)(2,1)S(1)}, bf16[512,512]{1,0:T(8,128)(2,1)S(1)}, u32[]{:S(2)}, u32[]{:S(2)}) collective-permute-start(bf16[512,512]{1,0:T(8,128)(2,1)S(1)} %get-tuple-element.52.refs_7_.refs_9_), channel_id=1, source_target_pairs={{0,4},{2,6},{4,0},{6,2},{8,12},{10,14},{12,8},{14,10},{16,20},{18,... | collective-permute-start | bytes 1572872 | tf_op jit(solution)/shard_map/ppermute | solution.py:24
  45.5 36.2 %collective-permute-start.6 = (bf16[512,512]{1,0:T(8,128)(2,1)S(1)}, bf16[512,512]{1,0:T(8,128)(2,1)S(1)}, u32[]{:S(2)}, u32[]{:S(2)}) collective-permute-start(bf16[512,512]{1,0:T(8,128)(2,1)S(1)} %collective-permute-done.4.refs_7_.refs_9_), channel_id=1, source_target_pairs={{4,0},{6,2},{12,8},{14,10},{20,16},{22,18},{28,24},{30,26},{5,1},{... | collective-permute-start | bytes 1572872 | tf_op jit(solution)/shard_map/ppermute | solution.py:24
  46.8 34.9 %collective-permute-start.7 = (bf16[256,512]{1,0:T(8,128)(2,1)S(1)}, bf16[256,512]{1,0:T(8,128)(2,1)S(1)}, u32[]{:S(2)}, u32[]{:S(2)}) collective-permute-start(bf16[256,512]{1,0:T(8,128)(2,1)S(1)} %get-tuple-element.58), channel_id=1, source_target_pairs={{0,20},{2,22},{4,24},{6,26},{8,28},{10,30},{1,21},{3,23},{5,25},{7... | collective-permute-start | bytes 786440 | tf_op jit(solution)/shard_map/ppermute | solution.py:24
  92.0 10.6 %collective-permute-start.9 = (bf16[256,2048]{1,0:T(8,128)(2,1)S(1)}, bf16[256,2048]{1,0:T(8,128)(2,1)S(1)}, u32[]{:S(2)}, u32[]{:S(2)}) collective-permute-start(bf16[256,2048]{1,0:T(8,128)(2,1)S(1)} %get-tuple-element.70), channel_id=1, source_target_pairs={{0,2},{2,0},{4,6},{6,4},{8,10},{10,8},{12,14},{14,12},{16,18},{18,... | collective-permute-start | bytes 3145736 | tf_op jit(solution)/shard_map/ppermute | solution.py:24
  105.1 12.7 %collective-permute-start.10 = (bf16[256,512]{1,0:T(8,128)(2,1)}, bf16[256,512]{1,0:T(8,128)(2,1)S(1)}, u32[]{:S(2)}, u32[]{:S(2)}) collective-permute-start(bf16[256,512]{1,0:T(8,128)(2,1)} %get-tuple-element.72), channel_id=1, source_target_pairs={{0,1},{1,0},{2,3},{3,2},{4,5},{5,4},{6,7},{7,6},{8,9},{9,8},{10,11... | collective-permute-start | bytes 786440 | tf_op jit(solution)/shard_map/ppermute | solution.py:523
  110.3 15.4 %collective-permute-start.11 = (bf16[256,1024]{1,0:T(8,128)(2,1)}, bf16[256,1024]{1,0:T(8,128)(2,1)S(1)}, u32[]{:S(2)}, u32[]{:S(2)}) collective-permute-start(bf16[256,1024]{1,0:T(8,128)(2,1)} %get-tuple-element.75), channel_id=1, source_target_pairs={{0,1},{1,0},{2,3},{3,2},{4,5},{5,4},{6,7},{7,6},{8,9},{9,8},{10,11... | collective-permute-start | bytes 1572872 | tf_op jit(solution)/shard_map/ppermute | solution.py:523
  112.6 18.3 %collective-permute-start.12 = (bf16[256,512]{1,0:T(8,128)(2,1)S(1)}, bf16[256,512]{1,0:T(8,128)(2,1)S(1)}, u32[]{:S(2)}, u32[]{:S(2)}) collective-permute-start(bf16[256,512]{1,0:T(8,128)(2,1)S(1)} %get-tuple-element.78), channel_id=1, source_target_pairs={{0,1},{1,0},{2,3},{3,2},{4,5},{5,4},{6,7},{7,6},{8,9},{9,8},{10,11... | collective-permute-start | bytes 786440 | tf_op jit(solution)/shard_map/ppermute | solution.py:523
where the time goes:
time: 131 us; the launch traced here: 132 us
  Pallas kernels  109 us (83%)
  starting transfers between devices  16.9 us (13%)
  waiting for transfers between devices  3.15 us (2%)
    pallas_call x5, Pallas kernels, attend(): pl.pallas_call(functools.partial(attend_body, spans=spans, arrays=len(pie...  81.4 us
    pallas_call x3, Pallas kernels, project(): pl.pallas_call(project_body, out_shape=jax.ShapeDtypeStruct((rows, chosen...  13.3 us
    ppermute x10, starting transfers between devices, shift(): lax.ppermute(array, 'ctx', [(i, j) for i, j in pairs if j is not None and...  13.2 us
    pallas_call x3, Pallas kernels, project_held(): pl.pallas_call(functools.partial(project_held_body, at=at, tile=min(256,...  7.96 us
    ppermute x3, starting transfers between devices, on_device(): arrived.append(lax.ppermute(sent, 'head', [(0, 1), (1, 0)]))  3.61 us
  transfers between devices with their start and end apart: 13, of which 3 were waited for; matrix products, arithmetic and copies ran while one was open for 2% of the time, Pallas kernels for 71%

commit v1 on v0

--- a/solution.py
+++ b/solution.py
@@ -110,10 +110,10 @@
     )(ids, mine, other)
 
 
-def attend_body(*refs, spans, arrays, group, heads, which, first, fetch, carried, final):
+def attend_body(*refs, q_count, spans, arrays, group, heads, which, first, fetch, carried, final):
     ids, lows, highs = refs[:3]
-    q_own, q_got, start_ref = refs[3:6]
-    refs = refs[6:]
+    sources, start_ref = refs[3 : 3 + q_count], refs[3 + q_count]
+    refs = refs[4 + q_count :]
     keys, vals, refs = refs[:arrays], refs[arrays : 2 * arrays], refs[2 * arrays + carried :]
     if fetch:
         weight, refs = refs[0], refs[1:]
@@ -127,7 +127,7 @@
 
     here = ids[0]
     core, column = here % 2, here // 2 % 2
-    rows = q_own.shape[0]
+    rows = sources[0].shape[0]
     h = pl.program_id(0)
     t = {"both": lambda: pl.program_id(1), "own": lambda: core, "other": lambda: 1 - core}[which]()
     chip_base = (here - core) * rows
@@ -146,15 +146,13 @@
 
     @pl.when(functools.reduce(jnp.logical_or, runs))
     def _():
-        @pl.when(t == core)
-        def _():
-            for g in range(group):
-                q[g] = q_own[:, g * HD : (g + 1) * HD]
-
-        @pl.when(t != core)
-        def _():
-            for g in range(group):
-                q[g] = q_got[:, g * HD : (g + 1) * HD]
+        for i, source in enumerate(sources):
+            here_or_there = (t == core) == (i == 0) if q_count == 2 else True
+
+            @pl.when(here_or_there)
+            def _(source=source):
+                for g in range(group):
+                    q[g] = source[:, g * HD : (g + 1) * HD]
 
     def turned(i):
         array, at, width, _ = spans[i]
@@ -297,14 +295,14 @@
     def tile_of(t, ids):
         return {"both": t, "own": ids[0] % 2, "other": 1 - ids[0] % 2}[which]
 
-    in_specs = [
-        pl.BlockSpec((rows, width), lambda h, t, i, *_: (0, i[0] % 2 * heads + h)),
-        pl.BlockSpec((rows, width), lambda h, t, *_: (0, h)),
-        pl.BlockSpec((1, 1, rows), lambda h, t, i, *_: (tile_of(t, i), 0, 0)),
-    ]
+    own_queries = (in_hbm(queries), pl.BlockSpec((rows, width), lambda h, t, i, *_: (0, i[0] % 2 * heads + h)))
+    other_queries = (got_queries, pl.BlockSpec((rows, width), lambda h, t, *_: (0, h)))
+    sources = {"both": [own_queries, other_queries], "own": [own_queries], "other": [other_queries]}[which]
+    in_specs = [spec for _, spec in sources]
+    in_specs.append(pl.BlockSpec((1, 1, rows), lambda h, t, i, *_: (tile_of(t, i), 0, 0)))
     in_specs += [pl.BlockSpec((p.shape[0], HD), lambda h, t, *_: (0, h)) for p in pieces]
     in_specs += [pl.BlockSpec((p.shape[0], HD), lambda h, t, *_: (0, heads + h)) for p in pieces]
-    operands = [*scalars, in_hbm(queries), got_queries, starts, *pieces, *pieces]
+    operands = [*scalars, *(array for array, _ in sources), starts, *pieces, *pieces]
     out_shape = [
         VMEM((heads, 2, group, rows, 2 * HD), jnp.float32),
         VMEM((heads, 2, group, rows, HD), jnp.float32),
@@ -336,6 +334,7 @@
     return pl.pallas_call(
         functools.partial(
             attend_body,
+            q_count=len(sources),
             spans=spans,
             arrays=len(pieces),
             group=group,
@@ -461,12 +460,7 @@
     sibling = functools.partial(shift, count=count, partner=lambda i: i ^ 1)
     mine, send, sent_queries = pack(ids, key_rows, values, queries, split)
     swapped = sibling(send)
-    up_level = functools.partial(shift, count=count, partner=lambda i: i + 4)
-    first_hop = [up_level(mine), up_level(swapped)]
-    own, upper = join(ids, mine, swapped)
-    sent_queries, lengths, mask_lo, _ = lax.optimization_barrier((sent_queries, lengths, mask_lo, swapped))
-    got_queries = sibling(sent_queries)
-
+    lengths, mask_lo, _ = lax.optimization_barrier((lengths, mask_lo, send))
     chip_base = (here - core) * rows
     doc_ends = jnp.cumsum(lengths)
     pos = chip_base + jnp.arange(2 * rows, dtype=jnp.int32)
@@ -475,6 +469,14 @@
     starts = jnp.maximum(doc_start, jnp.repeat(low, BLK)).astype(jnp.int32).reshape(2, rows)
     scalars = (ids, jnp.min(starts, axis=1), jnp.max(starts, axis=1))
     start_rows = starts[:, None, :]
+    swapped, start_rows, lows, highs = lax.optimization_barrier((swapped, start_rows, *scalars[1:]))
+    scalars = (ids, lows, highs)
+
+    up_level = functools.partial(shift, count=count, partner=lambda i: i + 4)
+    first_hop = [up_level(mine), up_level(swapped)]
+    own, upper = join(ids, mine, swapped)
+    sent_queries, _ = lax.optimization_barrier((sent_queries, swapped))
+    got_queries = sibling(sent_queries)
 
     common = (scalars, queries, got_queries, start_rows)
     near = shift(own, count, lambda i: i + 2 if i // 2 % 2 == 0 else None)
@@ -503,7 +505,7 @@
             upper, _ = lax.optimization_barrier((upper, moving))
             farthest = shift(upper, count, lambda i: i + reach)
         spans = [(0, 0, 2 * rows, at_before), (1, 0, 2 * rows, at_level)]
-        fetch = (out_weight, held_columns) if d == levels else ()
+        fetch = (out_weight, held_columns) if d == 1 else ()
         state = attend(*common, [before, moving], spans, state, group, heads, "both", *fetch)
         before, at_before, moving = crossed, at_cross, onward
     at_farthest = lambda base, column, r: base - reach * r + r

time: 131 us -> 131 us (level)
  starting transfers between devices: 16.9 us -> 18.7 us
  waiting for transfers between devices: 3.15 us -> 1.64 us
    ppermute x10, starting transfers between devices: 13.2 us -> 15.1 us  [shift(): lax.ppermute(array, 'ctx', [(i, j) for i, j in pairs if j is not None and...]
    ppermute x10, waiting for transfers between devices: 1.55 us -> 0.03 us  [shift(): lax.ppermute(array, 'ctx', [(i, j) for i, j in pairs if j is not None and...]
  transfers between devices with their start and end apart: 13 -> 13, of which waited for: 3 -> 2; matrix products, arithmetic and copies ran while one was open for 2% -> 2% of each run, Pallas kernels for 71% -> 71%
where the time goes in v1:
time: 131 us
  Pallas kernels  108 us (82%)
  starting transfers between devices  18.7 us (14%)
  waiting for transfers between devices  1.64 us (1%)
    pallas_call x5, Pallas kernels, attend(): pl.pallas_call(functools.partial(attend_body, q_count=len(sources), spans...  80.6 us
    ppermute x10, starting transfers between devices, shift(): lax.ppermute(array, 'ctx', [(i, j) for i, j in pairs if j is not None and...  15.1 us
    pallas_call x3, Pallas kernels, project(): pl.pallas_call(project_body, out_shape=jax.ShapeDtypeStruct((rows, chosen...  13.3 us
    pallas_call x3, Pallas kernels, project_held(): pl.pallas_call(functools.partial(project_held_body, at=at, tile=min(256,...  7.96 us
    ppermute x3, starting transfers between devices, on_device(): arrived.append(lax.ppermute(sent, 'head', [(0, 1), (1, 0)]))  3.61 us
  transfers between devices with their start and end apart: 13, of which 2 were waited for; matrix products, arithmetic and copies ran while one was open for 2% of the time, Pallas kernels for 71%

profile of v1, /device:TPU:16, one launch (start us, length us, event | category | flops | bytes accessed | tf_op | source)
XLA Modules:
  0.0 131.1 jit_solution(14354431858051770132)
XLA Ops:
  0.0 2.0 %pack.1 = (bf16[256,512]{1,0:T(8,128)(2,1)S(1)}, bf16[256,512]{1,0:T(8,128)(2,1)S(1)}, bf16[256,2048]{1,0:T(8,128)(2,1)S(1)}) custom-call(s32[3]{0:T(128)S(1)} %compare_select_fusion.1.ids.refs_0_, bf16[256,512]{1,0:T(8,128)(2,1)} %key_rows.1, bf16[256,512]{1,0:T(8,128)(2,1)} %values.1, bf16[256,4096]{1,0:T(8,128)(2,1)} %refs_3_.7), custom_call_target="tpu_custom_call" | custom-call | tf_op jit(solution)/shard_map/pack/pallas_call | solution.py:64
  4.9 3.5 %collective-permute-start.1 = (bf16[256,512]{1,0:T(8,128)(2,1)S(1)}, bf16[256,512]{1,0:T(8,128)(2,1)S(1)}, u32[]{:S(2)}, u32[]{:S(2)}) collective-permute-start(bf16[256,512]{1,0:T(8,128)(2,1)S(1)} %get-tuple-element.53.mine), channel_id=1, source_target_pairs={{0,8},{2,10},{4,12},{6,14},{8,16},{10,18},{12,20},{14,22},{16,24},... | collective-permute-start | bytes 786440 | tf_op jit(solution)/shard_map/ppermute | solution.py:24
  8.4 1.9 %collective-permute-start.2 = (bf16[256,512]{1,0:T(8,128)(2,1)S(1)}, bf16[256,512]{1,0:T(8,128)(2,1)S(1)}, u32[]{:S(2)}, u32[]{:S(2)}) collective-permute-start(bf16[256,512]{1,0:T(8,128)(2,1)S(1)} %collective-permute-done.other), channel_id=1, source_target_pairs={{0,8},{2,10},{4,12},{6,14},{8,16},{10,18},{12,20},{14,22},{16,24},... | collective-permute-start | bytes 786440 | tf_op jit(solution)/shard_map/ppermute | solution.py:24
  10.9 3.4 %collective-permute-start.5 = (bf16[512,512]{1,0:T(8,128)(2,1)S(1)}, bf16[512,512]{1,0:T(8,128)(2,1)S(1)}, u32[]{:S(2)}, u32[]{:S(2)}) collective-permute-start(bf16[512,512]{1,0:T(8,128)(2,1)S(1)} %get-tuple-element.57.refs_6_.refs_7_), channel_id=1, source_target_pairs={{0,4},{2,6},{8,12},{10,14},{16,20},{18,22},{24,28},{26,30},{1,5},{... | collective-permute-start | bytes 1572872 | tf_op jit(solution)/shard_map/ppermute | solution.py:24
  14.4 7.9 %attend_both_512.1 = (f32[2,2,8,256,256]{4,3,2,1,0:T(8,128)S(1)}, f32[2,2,8,256,128]{4,3,2,1,0:T(8,128)S(1)}, f32[2,2,2,8,128]{4,3,2,1,0:T(8,128)S(1)}) custom-call(s32[3]{0:T(128)S(1)} %compare_select_fusion.1.ids.refs_0_, s32[2]{0:T(128)S(1)} %get-tuple-element.50.refs_1_, s32[2]{0:T(128)S(1)} %get-tuple-element.51.refs_2_, bf16[256,4096]{1,0:T(8,128)(2,1)} %refs_3_.7, ...), custom_call_target="tpu_custom_call" | custom-call | flops 1048576 | bytes 65536 | tf_op jit(solution)/shard_map/attend_both_512/pallas_call | solution.py:334
  22.3 1.3 join.3
  23.6 1.9 %collective-permute-start.4 = (bf16[512,512]{1,0:T(8,128)(2,1)S(1)}, bf16[512,512]{1,0:T(8,128)(2,1)S(1)}, u32[]{:S(2)}, u32[]{:S(2)}) collective-permute-start(bf16[512,512]{1,0:T(8,128)(2,1)S(1)} %get-tuple-element.61.refs_7_.refs_9_), channel_id=1, source_target_pairs={{0,8},{2,10},{4,12},{6,14},{8,16},{10,18},{12,20},{14,22},{16,24},... | collective-permute-start | bytes 1572872 | tf_op jit(solution)/shard_map/ppermute | solution.py:24
  25.5 1.5 %collective-permute-start.8 = (bf16[512,512]{1,0:T(8,128)(2,1)S(1)}, bf16[512,512]{1,0:T(8,128)(2,1)S(1)}, u32[]{:S(2)}, u32[]{:S(2)}) collective-permute-start(bf16[512,512]{1,0:T(8,128)(2,1)S(1)} %get-tuple-element.61.refs_7_.refs_9_), channel_id=1, source_target_pairs={{0,4},{2,6},{4,0},{6,2},{8,12},{10,14},{12,8},{14,10},{16,20},{18,... | collective-permute-start | bytes 1572872 | tf_op jit(solution)/shard_map/ppermute | solution.py:24
  27.0 18.8 %attend_both_1024.2 = (f32[2,2,8,256,256]{4,3,2,1,0:T(8,128)S(1)}, f32[2,2,8,256,128]{4,3,2,1,0:T(8,128)S(1)}, f32[2,2,2,8,128]{4,3,2,1,0:T(8,128)S(1)}, bf16[4096,2048]{1,0:T(8,128)(2,1)S(1)}) custom-call(s32[3]{0:T(128)S(1)} %compare_select_fusion.1.ids.refs_0_, ...), custom_call_target="tpu_custom_call", output_to_operand_aliasing={{0}: (10, {}), {1}: (11, {}), {2}: (12, {})} | custom-call | flops 1048576 | bytes 65536 | tf_op jit(solution)/shard_map/attend_both_1024/pallas_call | solution.py:334
  45.8 1.3 collective-permute-start.6
  47.1 0.9 collective-permute-start.7
  48.0 34.0 %attend_both_1024.3 = (f32[2,2,8,256,256]{4,3,2,1,0:T(8,128)S(1)}, f32[2,2,8,256,128]{4,3,2,1,0:T(8,128)S(1)}, f32[2,2,2,8,128]{4,3,2,1,0:T(8,128)S(1)}, bf16[4096,2048]{1,0:T(8,128)(2,1)S(1)}) custom-call(s32[3]{0:T(128)S(1)} %compare_select_fusion.1.ids.refs_0_, ...), custom_call_target="tpu_custom_call", output_to_operand_aliasing={{0}: (10, {}), {1}: (11, {}), {2}: (12, {}), {3}: (13, {})} | custom-call | flops 1048576 | bytes 65536 | tf_op jit(solution)/shard_map/attend_both_1024/pallas_call | solution.py:334
  82.0 9.5 %attend_other_768.1 = (f32[2,2,8,256,256]{4,3,2,1,0:T(8,128)S(1)}, f32[2,2,8,256,128]{4,3,2,1,0:T(8,128)S(1)}, f32[2,2,2,8,128]{4,3,2,1,0:T(8,128)S(1)}, bf16[40...) custom-call(s32[3]{0:T(128)S(1)} %compare_select_fusion.1.ids.refs_0, ...), custom_call_target="tpu_custom_call", output_to_operand_aliasing={{0}: (9, {}), {1}: (10, {}), {2}: (11, {}), {3}: (12, {})} | custom-call | flops 1048576 | bytes 65536 | tf_op jit(solution)/shard_map/attend_other_768/pallas_call | solution.py:334
  91.6 10.5 %attend_own_768.1 = (f32[2,2,8,256,256]{4,3,2,1,0:T(8,128)S(1)}, f32[2,2,8,256,128]{4,3,2,1,0:T(8,128)S(1)}, f32[2,2,2,8,128]{4,3,2,1,0:T(8,128)S(1)}, bf16[4096...) custom-call(s32[3]{0:T(128)S(1)} %compare_select_fusion.1.ids.refs_0, ...), custom_call_target="tpu_custom_call", output_to_operand_aliasing={{0}: (9, {}), {1}: (10, {}), {2}: (11, {}), {3}: (12, {})} | custom-call | flops 1048576 | bytes 65536 | tf_op jit(solution)/shard_map/attend_own_768/pallas_call | solution.py:334
  102.1 2.5 %project_held.3 = (bf16[4096,2048]{1,0:T(8,128)(2,1)S(1)}, bf16[256,512]{1,0:T(8,128)(2,1)}) custom-call(s32[3]{0:T(128)S(1)} %compare_select_fusion.1.ids.refs_0_, bf16[256,2048]{1,0:T(8,128)(2,1)S(1)} %get-tuple-element.79.a_ref, bf16[256,2048]{1,0:T(8,128)(2,1)S(1)} %collective-permute-done.9.b_ref, ...), custom_call_target="tpu_custom_call", output_to_operand_aliasing={{0}: (3, {})} | custom-call | flops 1073741824 | bytes 67108864 | tf_op jit(solution)/shard_map/project_held/pallas_call | solution.py:378
  104.6 1.5 %collective-permute-start.10 = (bf16[256,512]{1,0:T(8,128)(2,1)}, bf16[256,512]{1,0:T(8,128)(2,1)S(1)}, u32[]{:S(2)}, u32[]{:S(2)}) collective-permute-start(bf16[256,512]{1,0:T(8,128)(2,1)} %get-tuple-element.82), channel_id=1, source_target_pairs={{0,1},{1,0},{2,3},{3,2},{4,5},{5,4},{6,7},{7,6},{8,9},{9,8},{10,11... | collective-permute-start | bytes 786440 | tf_op jit(solution)/shard_map/ppermute | solution.py:525
  106.1 3.7 %project_held.4 = (bf16[4096,2048]{1,0:T(8,128)(2,1)S(1)}, bf16[256,1024]{1,0:T(8,128)(2,1)}) custom-call(s32[3]{0:T(128)S(1)} %compare_select_fusion.1.ids.refs_0_, bf16[256,2048]{1,0:T(8,128)(2,1)S(1)} %get-tuple-element.79.a_ref, bf16[256,2048]{1,0:T(8,128)(2,1)S(1)} %collective-permute-done.9.b_ref, ...), custom_call_target="tpu_custom_call", output_to_operand_aliasing={{0}: (3, {})} | custom-call | flops 2147483648 | bytes 67108864 | tf_op jit(solution)/shard_map/project_held/pallas_call | solution.py:378
  110.3 1.8 %project_held.5 = (bf16[4096,2048]{1,0:T(8,128)(2,1)S(1)}, bf16[256,512]{1,0:T(8,128)(2,1)S(1)}) custom-call(s32[3]{0:T(128)S(1)} %compare_select_fusion.1.ids.refs_0_, bf16[256,2048]{1,0:T(8,128)(2,1)S(1)} %get-tuple-element.79.a_ref, bf16[256,2048]{1,0:T(8,128)(2,1)S(1)} %collective-permute-done.9.b_ref, ...), custom_call_target="tpu_custom_call", output_to_operand_aliasing={{0}: (3, {})} | custom-call | flops 1073741824 | bytes 67108864 | tf_op jit(solution)/shard_map/project_held/pallas_call | solution.py:378
  112.1 1.6 %collective-permute-start.12 = (bf16[256,512]{1,0:T(8,128)(2,1)S(1)}, bf16[256,512]{1,0:T(8,128)(2,1)S(1)}, u32[]{:S(2)}, u32[]{:S(2)}) collective-permute-start(bf16[256,512]{1,0:T(8,128)(2,1)S(1)} %get-tuple-element.88), channel_id=1, source_target_pairs={{0,1},{1,0},{2,3},{3,2},{4,5},{5,4},{6,7},{7,6},{8,9},{9,8},{10,11... | collective-permute-start | bytes 786440 | tf_op jit(solution)/shard_map/ppermute | solution.py:525
  113.7 3.6 %project.3.kept = bf16[256,512]{1,0:T(8,128)(2,1)S(1)} custom-call(s32[3]{0:T(128)S(1)} %compare_select_fusion.1.ids.refs_0_, bf16[256,2048]{1,0:T(8,128)(2,1)S(1)} %get-tuple-element.79.a_ref, bf16[256,2048]{1,0:T(8,128)(2,1)S(1)} %collective-permute-done.9.b_ref, bf16[4096,4096]{1,0:T(8,128)(2,1)} %wb_ref.5, bf16[4096,4096]{1,0:T(8,128)(2,1)} %wb_ref.5), custom_call_target="tpu_custom_call" | custom-call | flops 1048576 | bytes 65536 | tf_op jit(solution)/shard_map/project/pallas_call | solution.py:404
  118.1 6.1 %project.4.kept = bf16[256,1024]{1,0:T(8,128)(2,1)S(1)} custom-call(s32[3]{0:T(128)S(1)} %compare_select_fusion.1.ids.refs_0_, bf16[256,2048]{1,0:T(8,128)(2,1)S(1)} %get-tuple-element.79.a_ref, bf16[256,2048]{1,0:T(8,128)(2,1)S(1)} %collective-permute-done.9.b_ref, bf16[4096,4096]{1,0:T(8,128)(2,1)} %wb_ref.5, bf16[4096,4096]{1,0:T(8,128)(2,1)} %wb_ref.5), custom_call_target="tpu_custom_call" | custom-call | flops 17179869184 | bytes 134217728 | tf_op jit(solution)/shard_map/project/pallas_call | solution.py:404
  124.2 1.0 collective-permute-done.11.arrived
  125.1 0.9 add_columns.4.refs_0_
  126.1 3.6 %project.5.kept = bf16[256,512]{1,0:T(8,128)(2,1)S(1)} custom-call(s32[3]{0:T(128)S(1)} %compare_select_fusion.1.ids.refs_0_, bf16[256,2048]{1,0:T(8,128)(2,1)S(1)} %get-tuple-element.79.a_ref, bf16[256,2048]{1,0:T(8,128)(2,1)S(1)} %collective-permute-done.9.b_ref, bf16[4096,4096]{1,0:T(8,128)(2,1)} %wb_ref.5, bf16[4096,4096]{1,0:T(8,128)(2,1)} %wb_ref.5), custom_call_target="tpu_custom_call" | custom-call | flops 17179869184 | bytes 134217728 | tf_op jit(solution)/shard_map/project/pallas_call | solution.py:404
  (33 shorter events, 6.2 us)
Async XLA Ops:
  2.0 2.4 %collective-permute-start = (bf16[256,512]{1,0:T(8,128)(2,1)S(1)}, bf16[256,512]{1,0:T(8,128)(2,1)S(1)}, u32[]{:S(2)}, u32[]{:S(2)}) collective-permute-start(bf16[256,512]{1,0:T(8,128)(2,1)S(1)} %get-tuple-element.47), channel_id=1, source_target_pairs={{0,2},{2,0},{4,6},{6,4},{8,10},{10,8},{12,14},{14,12},{16,18},{18,... | collective-permute-start | bytes 786440 | tf_op jit(solution)/shard_map/ppermute | solution.py:24
  4.4 10.0 %collective-permute-start.3 = (bf16[256,2048]{1,0:T(8,128)(2,1)S(1)}, bf16[256,2048]{1,0:T(8,128)(2,1)S(1)}, u32[]{:S(2)}, u32[]{:S(2)}) collective-permute-start(bf16[256,2048]{1,0:T(8,128)(2,1)S(1)} %get-tuple-element.56), channel_id=1, source_target_pairs={{0,2},{2,0},{4,6},{6,4},{8,10},{10,8},{12,14},{14,12},{16,18},{18,... | collective-permute-start | bytes 3145736 | tf_op jit(solution)/shard_map/ppermute | solution.py:24
  4.9 17.4 %collective-permute-start.1 = (bf16[256,512]{1,0:T(8,128)(2,1)S(1)}, bf16[256,512]{1,0:T(8,128)(2,1)S(1)}, u32[]{:S(2)}, u32[]{:S(2)}) collective-permute-start(bf16[256,512]{1,0:T(8,128)(2,1)S(1)} %get-tuple-element.53.mine), channel_id=1, source_target_pairs={{0,8},{2,10},{4,12},{6,14},{8,16},{10,18},{12,20},{14,22},{16,24},... | collective-permute-start | bytes 786440 | tf_op jit(solution)/shard_map/ppermute | solution.py:24
  8.4 13.9 %collective-permute-start.2 = (bf16[256,512]{1,0:T(8,128)(2,1)S(1)}, bf16[256,512]{1,0:T(8,128)(2,1)S(1)}, u32[]{:S(2)}, u32[]{:S(2)}) collective-permute-start(bf16[256,512]{1,0:T(8,128)(2,1)S(1)} %collective-permute-done.other), channel_id=1, source_target_pairs={{0,8},{2,10},{4,12},{6,14},{8,16},{10,18},{12,20},{14,22},{16,24},... | collective-permute-start | bytes 786440 | tf_op jit(solution)/shard_map/ppermute | solution.py:24
  10.9 16.1 %collective-permute-start.5 = (bf16[512,512]{1,0:T(8,128)(2,1)S(1)}, bf16[512,512]{1,0:T(8,128)(2,1)S(1)}, u32[]{:S(2)}, u32[]{:S(2)}) collective-permute-start(bf16[512,512]{1,0:T(8,128)(2,1)S(1)} %get-tuple-element.57.refs_6_.refs_7_), channel_id=1, source_target_pairs={{0,4},{2,6},{8,12},{10,14},{16,20},{18,22},{24,28},{26,30},{1,5},{... | collective-permute-start | bytes 1572872 | tf_op jit(solution)/shard_map/ppermute | solution.py:24
  23.6 22.2 %collective-permute-start.4 = (bf16[512,512]{1,0:T(8,128)(2,1)S(1)}, bf16[512,512]{1,0:T(8,128)(2,1)S(1)}, u32[]{:S(2)}, u32[]{:S(2)}) collective-permute-start(bf16[512,512]{1,0:T(8,128)(2,1)S(1)} %get-tuple-element.61.refs_7_.refs_9_), channel_id=1, source_target_pairs={{0,8},{2,10},{4,12},{6,14},{8,16},{10,18},{12,20},{14,22},{16,24},... | collective-permute-start | bytes 1572872 | tf_op jit(solution)/shard_map/ppermute | solution.py:24
  25.5 22.5 %collective-permute-start.8 = (bf16[512,512]{1,0:T(8,128)(2,1)S(1)}, bf16[512,512]{1,0:T(8,128)(2,1)S(1)}, u32[]{:S(2)}, u32[]{:S(2)}) collective-permute-start(bf16[512,512]{1,0:T(8,128)(2,1)S(1)} %get-tuple-element.61.refs_7_.refs_9_), channel_id=1, source_target_pairs={{0,4},{2,6},{4,0},{6,2},{8,12},{10,14},{12,8},{14,10},{16,20},{18,... | collective-permute-start | bytes 1572872 | tf_op jit(solution)/shard_map/ppermute | solution.py:24
  45.8 36.2 %collective-permute-start.6 = (bf16[512,512]{1,0:T(8,128)(2,1)S(1)}, bf16[512,512]{1,0:T(8,128)(2,1)S(1)}, u32[]{:S(2)}, u32[]{:S(2)}) collective-permute-start(bf16[512,512]{1,0:T(8,128)(2,1)S(1)} %collective-permute-done.4.refs_7_.refs_9_), channel_id=1, source_target_pairs={{4,0},{6,2},{12,8},{14,10},{20,16},{22,18},{28,24},{30,26},{5,1},{... | collective-permute-start | bytes 1572872 | tf_op jit(solution)/shard_map/ppermute | solution.py:24
  47.1 34.9 %collective-permute-start.7 = (bf16[256,512]{1,0:T(8,128)(2,1)S(1)}, bf16[256,512]{1,0:T(8,128)(2,1)S(1)}, u32[]{:S(2)}, u32[]{:S(2)}) collective-permute-start(bf16[256,512]{1,0:T(8,128)(2,1)S(1)} %get-tuple-element.67), channel_id=1, source_target_pairs={{0,20},{2,22},{4,24},{6,26},{8,28},{10,30},{1,21},{3,23},{5,25},{7... | collective-permute-start | bytes 786440 | tf_op jit(solution)/shard_map/ppermute | solution.py:24
  91.5 10.6 %collective-permute-start.9 = (bf16[256,2048]{1,0:T(8,128)(2,1)S(1)}, bf16[256,2048]{1,0:T(8,128)(2,1)S(1)}, u32[]{:S(2)}, u32[]{:S(2)}) collective-permute-start(bf16[256,2048]{1,0:T(8,128)(2,1)S(1)} %get-tuple-element.80), channel_id=1, source_target_pairs={{0,2},{2,0},{4,6},{6,4},{8,10},{10,8},{12,14},{14,12},{16,18},{18,... | collective-permute-start | bytes 3145736 | tf_op jit(solution)/shard_map/ppermute | solution.py:24
  104.6 12.7 %collective-permute-start.10 = (bf16[256,512]{1,0:T(8,128)(2,1)}, bf16[256,512]{1,0:T(8,128)(2,1)S(1)}, u32[]{:S(2)}, u32[]{:S(2)}) collective-permute-start(bf16[256,512]{1,0:T(8,128)(2,1)} %get-tuple-element.82), channel_id=1, source_target_pairs={{0,1},{1,0},{2,3},{3,2},{4,5},{5,4},{6,7},{7,6},{8,9},{9,8},{10,11... | collective-permute-start | bytes 786440 | tf_op jit(solution)/shard_map/ppermute | solution.py:525
  109.8 15.4 %collective-permute-start.11 = (bf16[256,1024]{1,0:T(8,128)(2,1)}, bf16[256,1024]{1,0:T(8,128)(2,1)S(1)}, u32[]{:S(2)}, u32[]{:S(2)}) collective-permute-start(bf16[256,1024]{1,0:T(8,128)(2,1)} %get-tuple-element.85), channel_id=1, source_target_pairs={{0,1},{1,0},{2,3},{3,2},{4,5},{5,4},{6,7},{7,6},{8,9},{9,8},{10,11... | collective-permute-start | bytes 1572872 | tf_op jit(solution)/shard_map/ppermute | solution.py:525
  112.1 18.3 %collective-permute-start.12 = (bf16[256,512]{1,0:T(8,128)(2,1)S(1)}, bf16[256,512]{1,0:T(8,128)(2,1)S(1)}, u32[]{:S(2)}, u32[]{:S(2)}) collective-permute-start(bf16[256,512]{1,0:T(8,128)(2,1)S(1)} %get-tuple-element.88), channel_id=1, source_target_pairs={{0,1},{1,0},{2,3},{3,2},{4,5},{5,4},{6,7},{7,6},{8,9},{9,8},{10,11... | collective-permute-start | bytes 786440 | tf_op jit(solution)/shard_map/ppermute | solution.py:525
